TPU v7x, 256 devices: a whole 4x4x8 slice. The times are simulated.
256 devices in a mesh: dp: 256 (over x, y, z, core).
Axes of the slice: x: 4, y: 4, z: 8, core: 2. Of those that a mesh axis runs over, the one named last changes fastest.
Arguments:
- picture_embedding_matrix: float32 [131072, 1152], P('dp'), may hold values from -1.0298836 to 1.0298836
- caption_embedding_matrix: float32 [131072, 1152], P('dp'), may hold values from -1.0298836 to 1.0298836
- sharpness_factor: float32 [1], replicated, may hold values from 0.5 to 2
- offset_term: float32 [1], replicated, may hold values from -4 to -1
Outputs:
- picture_embedding_derivative: float32 [131072, 1152], P('dp')
- text_gradient: float32 [131072, 1152], P('dp')
All inputs are finite; a program needn't handle non-finite values.
Results may differ from a plain program's by a relative error of at most 0.00011.
Values sent between devices are 32-bit elements; how exact they have to be, the bound alone decides.
A program may use at most 64 MiB of HBM per device.

v0:
```python
import functools

import jax
import jax.numpy as jnp
from jax import lax
from jax.experimental import pallas as pl
from jax.experimental.pallas import tpu as pltpu
from jax.sharding import PartitionSpec as P

MESH = pl.DeviceIdType.MESH
F32 = jnp.float32
BF16 = jnp.bfloat16

V, U, NEAR, A2, B2, PFB, PFA, Q3 = range(8)
CHUNKS = 4
HALVES = 2


def split(x):
    high = x.astype(BF16)
    return high, (x - high.astype(F32)).astype(BF16)


def dot_nt(a, b):
    return lax.dot_general(a, b, (((1,), (1,)), ((), ())), preferred_element_type=F32)


def dot_nn(a, b):
    return lax.dot_general(a, b, (((1,), (0,)), ((), ())), preferred_element_type=F32)


def kernel(n, scale_ref, offset_ref, img, txt, img_grad, txt_grad, buf, high, low, acc, load_sem, out_sem, send_sem, recv_sem):
    rows = img.shape[0]
    chunk = rows // CHUNKS
    half = rows // HALVES
    me = lax.axis_index("dp")
    odd = lax.rem(me, 2)
    e = 2 * odd - 1
    scale = scale_ref[0]
    offset = offset_ref[0]

    def device(distance):
        return (lax.rem(me + distance + n, n),)

    def by_core(do):
        @pl.when(odd == 1)
        def _():
            do(img, txt, img_grad, txt_grad)

        @pl.when(odd == 0)
        def _():
            do(txt, img, txt_grad, img_grad)

    def copy(kind, c, src, to, distance):
        part = pl.ds(c * chunk, chunk)
        return pltpu.make_async_remote_copy(
            src_ref=src.at[part],
            dst_ref=buf.at[to, part],
            send_sem=send_sem.at[kind, c],
            recv_sem=recv_sem.at[kind, c],
            device_id=device(distance),
            device_id_type=MESH,
        )

    def near(c, u):
        return copy(0, c, u, NEAR, -e)

    def a2(c, v):
        return copy(1, c, v, A2, 2 * e)

    def b2(c, u):
        return copy(2, c, u, B2, -2 * e)

    def pfb(c):
        return copy(3, c, buf.at[B2], PFB, -e)

    def pfa(c):
        return copy(4, c, buf.at[A2], PFA, -e)

    def q3(c):
        return copy(5, c, buf.at[A2], Q3, e)

    def load(u, v, *_):
        pltpu.make_async_copy(v, buf.at[V], load_sem.at[0]).start()
        pltpu.make_async_copy(u, buf.at[U], load_sem.at[1]).start()

    by_core(load)
    barrier = pltpu.get_barrier_semaphore()
    for distance in (-2, -1, 1, 2):
        pl.semaphore_signal(barrier, inc=1, device_id=device(distance), device_id_type=MESH)
    pl.semaphore_wait(barrier, 4)

    def send(u, v, *_):
        for c in range(CHUNKS):
            a2(c, v).start()
            b2(c, u).start()
        for c in range(CHUNKS):
            near(c, u).start()

    by_core(send)

    for k, block in enumerate((V, U)):
        pltpu.make_async_copy(img, buf.at[block], load_sem.at[k]).wait()
    for k, block in enumerate((U, V)):
        h, l = split(buf[block])
        high[k] = h
        low[k] = l
    acc[...] = jnp.zeros_like(acc)

    def score(block, start, size, k, diagonal):
        xh, xl = split(buf[block, pl.ds(start, size), :])
        for m in range(0, rows, 256):
            at = pl.ds(m, 256)
            ah, al = high[k, at, :], low[k, at, :]
            z = scale * (dot_nt(ah, xh) + (dot_nt(ah, xl) + dot_nt(al, xh))) + offset
            if diagonal:
                row = lax.broadcasted_iota(jnp.int32, z.shape, 0) + m
                column = lax.broadcasted_iota(jnp.int32, z.shape, 1) + start
                sign = jnp.where((row == column) & (block < NEAR), -1.0, 1.0)
                p = scale * (sign * lax.logistic(sign * z))
            else:
                p = scale * lax.logistic(z)
            ph, pl_ = split(p)
            acc[k, at, :] += dot_nn(ph, xh) + (dot_nn(ph, xl) + dot_nn(pl_, xh))

    def first(t, _):
        block = t // HALVES

        @pl.when(t == NEAR * HALVES)
        def _():
            for c in range(CHUNKS):
                near(c, img).wait_recv()

        score(block, pl.multiple_of(lax.rem(t, HALVES) * half, half), half, lax.rem(block, 2), True)
        return 0

    lax.fori_loop(0, 3 * HALVES, first, 0)

    per = CHUNKS // HALVES

    def second(t, _):
        part, which = t // 4, lax.rem(t, 4)

        @pl.when(which == 0)
        def _():
            for i in range(per):
                c = part * per + i
                a2(c, txt).wait_recv()
                pfa(c).start()
                q3(c).start()
                b2(c, img).wait_recv()
                pfb(c).start()

        @pl.when(which == 2)
        def _():
            for i in range(per):
                pfb(part * per + i).wait_recv()

        @pl.when(which == 3)
        def _():
            for i in range(per):
                pfa(part * per + i).wait_recv()

        score(A2 + which, pl.multiple_of(part * half, half), half, lax.rem(which, 2), False)
        return 0

    lax.fori_loop(0, 4 * HALVES, second, 0)

    def store(k):
        def go(img_grad, txt_grad, u_grad, v_grad):
            pltpu.make_async_copy(acc.at[k], (u_grad, v_grad)[k], out_sem.at[k]).start()

        return go

    by_core(store(0))

    def third(c, _):
        q3(c).wait_recv()
        score(Q3, pl.multiple_of(c * chunk, chunk), chunk, 1, False)
        return 0

    lax.fori_loop(0, CHUNKS, third, 0)
    by_core(store(1))
    for c in range(CHUNKS):
        near(c, img).wait_send()
        a2(c, img).wait_send()
        b2(c, img).wait_send()
        pfb(c).wait_send()
        pfa(c).wait_send()
        q3(c).wait_send()
    for k in range(2):
        pltpu.make_async_copy(acc.at[k], img_grad, out_sem.at[k]).wait()


def local(img, txt, scale, offset):
    rows, width = img.shape
    n = lax.axis_size("dp")
    hbm = pl.BlockSpec(memory_space=pltpu.HBM)
    smem = pl.BlockSpec(memory_space=pltpu.SMEM)
    return pl.pallas_call(
        functools.partial(kernel, n),
        out_shape=[jax.ShapeDtypeStruct((rows, width), F32)] * 2,
        in_specs=[smem, smem, hbm, hbm],
        out_specs=[hbm, hbm],
        scratch_shapes=[
            pltpu.VMEM((8, rows, width), F32),
            pltpu.VMEM((2, rows, width), BF16),
            pltpu.VMEM((2, rows, width), BF16),
            pltpu.VMEM((2, rows, width), F32),
            pltpu.SemaphoreType.DMA((2,)),
            pltpu.SemaphoreType.DMA((2,)),
            pltpu.SemaphoreType.DMA((6, CHUNKS)),
            pltpu.SemaphoreType.DMA((6, CHUNKS)),
        ],
        compiler_params=pltpu.CompilerParams(
            collective_id=0, has_side_effects=True, vmem_limit_bytes=52 * 2**20
        ),
    )(scale, offset, img, txt)


def solution(mesh):
    placed = (P("dp", None), P("dp", None), P(), P())
    return jax.shard_map(
        local, mesh=mesh, in_specs=placed, out_specs=(P("dp", None), P("dp", None)), check_vma=False
    )
```

profile of v0, /device:TPU:0, one launch (start us, length us, event | category | flops | bytes accessed | tf_op | source)
XLA Modules:
  0.0 99.3 jit_solution(4292809585880309020)
XLA Ops:
  1.9 92.6 %shard_map.59 = (f32[512,1152]{1,0:T(8,128)}, f32[512,1152]{1,0:T(8,128)}) custom-call(f32[1]{0:T(128)S(6)} %copy.8.scale_ref, f32[1]{0:T(128)S(6)} %copy.9.offset_ref, f32[512,1152]{1,0:T(8,128)} %img.1, f32[512,1152]{1,0:T(8,128)} %txt.1), custom_call_target="tpu_custom_call" | custom-call | tf_op jit(solution)/shard_map/pallas_call | solution.py:200
  94.5 0.0 copy-start
  94.5 3.4 %copy.10 = f32[512,1152]{1,0:T(8,128)} copy(f32[512,1152]{1,0:T(8,128)} %get-tuple-element.4) | data formatting | bytes 4718592
  97.9 0.0 copy-done
  97.9 1.4 %copy.11 = f32[512,1152]{1,0:T(8,128)} copy(f32[512,1152]{1,0:T(8,128)S(1)} %copy-done) | data formatting | bytes 4718592
Async XLA Ops:
  94.5 3.4 %copy-start = (f32[512,1152]{1,0:T(8,128)S(1)}, f32[512,1152]{1,0:T(8,128)}, u32[]{:S(2)}) copy-start(f32[512,1152]{1,0:T(8,128)} %get-tuple-element.5) | copy-start | bytes 7077892
where the time goes:
time: 100 us; the launch traced here: 99.3 us
  Pallas kernels  92.6 us (93%)
  local copies, waits for them, and re-layouts  4.78 us (5%)
  between operations  1.94 us (2%)
    pallas_call x1, Pallas kernels, local(): pl.pallas_call(functools.partial(kernel, n), out_shape=[jax.ShapeDtypeStr...  92.6 us
    unnamed x4, local copies, waits for them, and re-layouts  4.78 us

commit v1 on v0

v1 whole, which is shorter than its diff:
```python
import functools

import jax
import jax.numpy as jnp
from jax import lax
from jax.experimental import pallas as pl
from jax.experimental.pallas import tpu as pltpu
from jax.sharding import PartitionSpec as P

MESH = pl.DeviceIdType.MESH
F32 = jnp.float32
BF16 = jnp.bfloat16
HBM = pl.BlockSpec(memory_space=pltpu.HBM)
SMEM = pl.BlockSpec(memory_space=pltpu.SMEM)
VMEM = pl.BlockSpec(memory_space=pltpu.VMEM)

V, U, NEAR, A2, B2, PFB, PFA, Q3 = range(8)
HALVES = 2
SIZES = (64,) * 8
STARTS = tuple(sum(SIZES[:i]) for i in range(len(SIZES)))
PIECES = len(SIZES)
TAIL = ((0, 256, (0, 1, 2, 3)), (256, 128, (4, 5)), (384, 64, (6,)))


def split(x):
    high = x.astype(BF16)
    return high, (x - high.astype(F32)).astype(BF16)


def dot_nt(a, b):
    return lax.dot_general(a, b, (((1,), (1,)), ((), ())), preferred_element_type=F32)


def dot_nn(a, b):
    return lax.dot_general(a, b, (((1,), (0,)), ((), ())), preferred_element_type=F32)


def similarity(ah, al, xh, xl):
    return dot_nt(ah, xh) + (dot_nt(ah, xl) + dot_nt(al, xh))


def weighted(ph, pl_, xh, xl):
    return dot_nn(ph, xh) + (dot_nn(ph, xl) + dot_nn(pl_, xh))


def weigh_small(scale, offset, ah, al, xh, xl):
    size = xh.shape[0]
    both = jnp.concatenate([xh, xl], axis=0)
    dots = dot_nt(ah, both)
    z = scale * (dots[:, :size] + (dots[:, size:] + dot_nt(al, xh))) + offset
    ph, pl_ = split(scale * lax.logistic(z))
    return dot_nn(jnp.concatenate([ph, ph, pl_], axis=1), jnp.concatenate([both, xh], axis=0))


def exchange(n, factors, img, txt, acc, high, low, tail, buf, dots, slopes, load_sem, send_sem, recv_sem):
    rows = img.shape[0]
    half = rows // HALVES
    me = lax.axis_index("dp")
    odd = lax.rem(me, 2)
    e = 2 * odd - 1

    def device(distance):
        return (lax.rem(me + distance + n, n),)

    def by_core(do):
        @pl.when(odd == 1)
        def _():
            do(img, txt)

        @pl.when(odd == 0)
        def _():
            do(txt, img)

    def copy(kind, c, src, to, distance):
        part = pl.ds(STARTS[c], SIZES[c])
        return pltpu.make_async_remote_copy(
            src_ref=src.at[part],
            dst_ref=tail if (to == Q3 and c == PIECES - 1) else buf.at[to, part],
            send_sem=send_sem.at[kind, c],
            recv_sem=recv_sem.at[kind, c],
            device_id=device(distance),
            device_id_type=MESH,
        )

    def near(u):
        return pltpu.make_async_remote_copy(
            src_ref=u,
            dst_ref=buf.at[NEAR],
            send_sem=send_sem.at[0, 0],
            recv_sem=recv_sem.at[0, 0],
            device_id=device(-e),
            device_id_type=MESH,
        )

    def a2(c, v):
        return copy(1, c, v, A2, 2 * e)

    def b2(c, u):
        return copy(2, c, u, B2, -2 * e)

    def pfb(c):
        return copy(3, c, buf.at[B2], PFB, -e)

    def pfa(c):
        return copy(4, c, buf.at[A2], PFA, -e)

    def q3(c):
        return copy(5, c, buf.at[A2], Q3, e)

    def load(u, v):
        pltpu.make_async_copy(v, buf.at[V], load_sem.at[0]).start()
        pltpu.make_async_copy(u, buf.at[U], load_sem.at[1]).start()

    by_core(load)
    barrier = pltpu.get_barrier_semaphore()
    for distance in (-2, -1, 1, 2):
        pl.semaphore_signal(barrier, inc=1, device_id=device(distance), device_id_type=MESH)
    pl.semaphore_wait(barrier, 4)

    def send(u, v):
        for c in range(PIECES):
            a2(c, v).start()
            b2(c, u).start()
        near(u).start()

    by_core(send)

    acc[...] = jnp.zeros_like(acc)
    scale = factors[0]
    offset = factors[1]
    for k, block in enumerate((V, U)):
        pltpu.make_async_copy(img, buf.at[block], load_sem.at[k]).wait()

    def own(which):
        return lax.rem(which + 1 + odd, 2)

    def prepare(t, _):
        at = pl.ds(pl.multiple_of(t * 128, 128), 128)
        for which, block in enumerate((U, V)):
            h, l = split(buf[block, at, :])
            high[own(which), at, :] = h
            low[own(which), at, :] = l
        return 0

    lax.fori_loop(0, rows // 128, prepare, 0)

    def score(block, start, size, which, diagonal):
        k = own(which)
        xh, xl = split(buf[block, pl.ds(start, size), :])
        for m in range(0, rows, 256):
            at = pl.ds(m, 256)
            dots[at, :size] = similarity(high[k, at, :], low[k, at, :], xh, xl)

        def slope(t, _):
            m = pl.multiple_of(t * 64, 64)
            at = pl.ds(m, 64)
            z = scale * dots[at, :size] + offset
            if diagonal:
                row = lax.broadcasted_iota(jnp.int32, z.shape, 0) + m
                column = lax.broadcasted_iota(jnp.int32, z.shape, 1) + start
                sign = jnp.where((row == column) & (block < NEAR), -1.0, 1.0)
                p = scale * (sign * lax.logistic(sign * z))
            else:
                p = scale * lax.logistic(z)
            ph, pl_ = split(p)
            slopes[0, at, :size] = ph
            slopes[1, at, :size] = pl_
            return 0

        lax.fori_loop(0, rows // 64, slope, 0)
        for m in range(0, rows, 256):
            at = pl.ds(m, 256)
            acc[k, at, :] += weighted(slopes[0, at, :size], slopes[1, at, :size], xh, xl)

    def score_small(block, start, size, which):
        k = own(which)
        xh, xl = split(buf[block, pl.ds(start, size), :])
        acc[k, ...] += weigh_small(scale, offset, high[k, ...], low[k, ...], xh, xl)

    def first(t, _):
        block = t // HALVES

        @pl.when(t == NEAR * HALVES)
        def _():
            near(img).wait_recv()

        score(block, pl.multiple_of(lax.rem(t, HALVES) * half, half), half, lax.rem(block, 2), True)
        return 0

    lax.fori_loop(0, 3 * HALVES, first, 0)

    def second(t, _):
        part, which = t // 4, lax.rem(t, 4)
        for h in range(HALVES):
            pieces = [c for c in range(PIECES) if STARTS[c] // half == h]

            @pl.when(t == 4 * h)
            def _():
                for c in pieces:
                    a2(c, txt).wait_recv()
                    q3(c).start()
                    pfa(c).start()
                    b2(c, img).wait_recv()
                    pfb(c).start()

            @pl.when(t == 4 * h + 2)
            def _():
                for c in pieces:
                    pfb(c).wait_recv()

            @pl.when(t == 4 * h + 3)
            def _():
                for c in pieces:
                    pfa(c).wait_recv()

        score(A2 + which, pl.multiple_of(part * half, half), half, lax.rem(which, 2), False)
        return 0

    lax.fori_loop(0, 4 * HALVES, second, 0)

    for start, size, pieces in TAIL:
        for c in pieces:
            q3(c).wait_recv()
        (score if size > 128 else score_small)(Q3, start, size, 1, *((False,) if size > 128 else ()))
    near(img).wait_send()
    for c in range(PIECES):
        a2(c, img).wait_send()
        b2(c, img).wait_send()
        pfb(c).wait_send()
        pfa(c).wait_send()
        q3(c).wait_send()
    q3(PIECES - 1).wait_recv()


def finish(factors, acc, high, low, tail, img_grad, txt_grad, result, out_sem):
    rows = high.shape[1]
    odd = lax.rem(lax.axis_index("dp"), 2)
    grads = (img_grad, txt_grad)
    scale = factors[0]
    offset = factors[1]
    done = [pltpu.make_async_copy(acc.at[k], grads[k], out_sem.at[0]) for k in range(2)]
    for k in range(2):
        pl.when(odd == 1 - k)(done[k].start)
    xh, xl = split(tail[...])
    step = 256
    for m in range(0, rows, step):
        at = pl.ds(m, step)
        result[at, :] = acc[odd, at, :] + weigh_small(scale, offset, high[odd, at, :], low[odd, at, :], xh, xl)
        for k in range(2):
            part = pltpu.make_async_copy(result.at[at], grads[k].at[at], out_sem.at[1 + m // step])
            pl.when(odd == k)(part.start)
    done[0].wait()
    for m in range(0, rows, step):
        at = pl.ds(m, step)
        pltpu.make_async_copy(result.at[at], img_grad.at[at], out_sem.at[1 + m // step]).wait()


def local(img, txt, scale, offset):
    rows, width = img.shape
    n = lax.axis_size("dp")
    factors = jnp.concatenate([scale, offset])
    img, txt = (pltpu.with_memory_space_constraint(x, pltpu.HBM) for x in (img, txt))
    kept = pl.pallas_call(
        functools.partial(exchange, n),
        out_shape=[
            pltpu.VMEM((2, rows, width), F32),
            pltpu.VMEM((2, rows, width), BF16),
            pltpu.VMEM((2, rows, width), BF16),
            pltpu.VMEM((SIZES[-1], width), F32),
        ],
        in_specs=[SMEM] + [HBM] * 2,
        out_specs=[VMEM] * 4,
        scratch_shapes=[
            pltpu.VMEM((8, rows, width), F32),
            pltpu.VMEM((rows, rows // HALVES), F32),
            pltpu.VMEM((2, rows, rows // HALVES), BF16),
            pltpu.SemaphoreType.DMA((2,)),
            pltpu.SemaphoreType.DMA((6, PIECES)),
            pltpu.SemaphoreType.DMA((6, PIECES)),
        ],
        compiler_params=pltpu.CompilerParams(collective_id=0, has_side_effects=True, vmem_limit_bytes=40 * 2**20),
    )(factors, img, txt)
    kept = [pltpu.with_memory_space_constraint(x, pltpu.VMEM) for x in kept]
    return pl.pallas_call(
        finish,
        out_shape=[jax.ShapeDtypeStruct((rows, width), F32)] * 2,
        in_specs=[SMEM] + [VMEM] * 4,
        out_specs=[HBM] * 2,
        scratch_shapes=[
            pltpu.VMEM((rows, width), F32),
            pltpu.SemaphoreType.DMA((5,)),
        ],
        compiler_params=pltpu.CompilerParams(vmem_limit_bytes=16 * 2**20),
    )(factors, *kept)


def solution(mesh):
    placed = (P("dp", None), P("dp", None), P(), P())
    return jax.shard_map(
        local, mesh=mesh, in_specs=placed, out_specs=(P("dp", None), P("dp", None)), check_vma=False
    )
```

time: 100 us -> 94.7 us (0.947)
  local copies, waits for them, and re-layouts: 4.78 us -> 0 us
  Pallas kernels: 92.6 us -> 91.2 us
    unnamed x4 -> x0, local copies, waits for them, and re-layouts: 4.78 us -> none
    pallas_call x1 -> x2, Pallas kernels: 92.6 us -> 91.2 us  [the longest x1 87.8 us: local(): pl.pallas_call(functools.partial(exchange, n), out_shape=[pltpu.VMEM((2,...]
where the time goes in v1:
time: 94.7 us; the launch traced here: 93.3 us
  Pallas kernels  91.2 us (96%)
  between operations  1.93 us (2%)
    pallas_call x1, Pallas kernels, local(): pl.pallas_call(functools.partial(exchange, n), out_shape=[pltpu.VMEM((2,...  87.8 us
    pallas_call x1, Pallas kernels, local(): pl.pallas_call(finish, out_shape=[jax.ShapeDtypeStruct((rows, width), F32...  3.46 us

profile of v1, /device:TPU:0, one launch (start us, length us, event | category | flops | bytes accessed | tf_op | source)
XLA Modules:
  0.0 93.3 jit_solution(15418636339487914292)
XLA Ops:
  1.9 0.1 pad_maximum_fusion.factors
  2.0 87.8 %shard_map.59 = (f32[2,512,1152]{2,1,0:T(8,128)S(1)}, bf16[2,512,1152]{2,1,0:T(8,128)(2,1)S(1)}, bf16[2,512,1152]{2,1,0:T(8,128)(2,1)S(1)}, f32[64,1152]{1,0:T(8,128)S(1)}) custom-call(f32[2]{0:T(128)S(1)} %pad_maximum_fusion.factors, f32[512,1152]{1,0:T(8,128)} %img.1, f32[512,1152]{1,0:T(8,128)} %txt.1), custom_call_target="tpu_custom_call" | custom-call | tf_op jit(solution)/shard_map/pallas_call | solution.py:263
  89.8 3.5 %shard_map.60 = (f32[512,1152]{1,0:T(8,128)}, f32[512,1152]{1,0:T(8,128)}) custom-call(f32[2]{0:T(128)S(1)} %pad_maximum_fusion.factors, f32[2,512,1152]{2,1,0:T(8,128)S(1)} %get-tuple-element.6.acc, bf16[2,512,1152]{2,1,0:T(8,128)(2,1)S(1)} %get-tuple-element.7.high, bf16[2,512,1152]{2,1,0:T(8,128)(2,1)S(1)} %get-tuple-element.8.low, ...), custom_call_target="tpu_custom_call" | custom-call | tf_op jit(solution)/shard_map/pallas_call | solution.py:284

commit v2 on v1

--- a/solution.py
+++ b/solution.py
@@ -52,7 +52,7 @@
     return dot_nn(jnp.concatenate([ph, ph, pl_], axis=1), jnp.concatenate([both, xh], axis=0))
 
 
-def exchange(n, factors, img, txt, acc, high, low, tail, buf, dots, slopes, load_sem, send_sem, recv_sem):
+def exchange(n, scale_ref, offset_ref, img, txt, acc, high, low, tail, buf, dots, slopes, entered, load_sem, send_sem, recv_sem):
     rows = img.shape[0]
     half = rows // HALVES
     me = lax.axis_index("dp")
@@ -111,23 +111,29 @@
         pltpu.make_async_copy(v, buf.at[V], load_sem.at[0]).start()
         pltpu.make_async_copy(u, buf.at[U], load_sem.at[1]).start()
 
+    barrier = pltpu.get_barrier_semaphore()
+    for distance in (-2, -1):
+        pl.semaphore_signal(barrier, inc=1, device_id=device(distance), device_id_type=MESH)
     by_core(load)
-    barrier = pltpu.get_barrier_semaphore()
-    for distance in (-2, -1, 1, 2):
-        pl.semaphore_signal(barrier, inc=1, device_id=device(distance), device_id_type=MESH)
-    pl.semaphore_wait(barrier, 4)
-
-    def send(u, v):
+    pl.semaphore_wait(barrier, 2)
+    for i in range(2):
+        pl.semaphore_signal(entered.at[i], inc=1, device_id=device(i + 1), device_id_type=MESH)
+
+    def send(u, v, upper):
         for c in range(PIECES):
-            a2(c, v).start()
-            b2(c, u).start()
-        near(u).start()
-
-    by_core(send)
+            (a2(c, v) if upper else b2(c, u)).start()
+
+    pl.when(odd == 1)(lambda: send(img, txt, True))
+    pl.when(odd == 0)(lambda: send(txt, img, False))
+    for i in range(2):
+        pl.semaphore_wait(entered.at[i], 1)
+    pl.when(odd == 1)(lambda: send(img, txt, False))
+    pl.when(odd == 0)(lambda: send(txt, img, True))
+    by_core(lambda u, v: near(u).start())
 
     acc[...] = jnp.zeros_like(acc)
-    scale = factors[0]
-    offset = factors[1]
+    scale = scale_ref[0]
+    offset = offset_ref[0]
     for k, block in enumerate((V, U)):
         pltpu.make_async_copy(img, buf.at[block], load_sem.at[k]).wait()
 
@@ -232,12 +238,12 @@
     q3(PIECES - 1).wait_recv()
 
 
-def finish(factors, acc, high, low, tail, img_grad, txt_grad, result, out_sem):
+def finish(scale_ref, offset_ref, acc, high, low, tail, img_grad, txt_grad, result, out_sem):
     rows = high.shape[1]
     odd = lax.rem(lax.axis_index("dp"), 2)
     grads = (img_grad, txt_grad)
-    scale = factors[0]
-    offset = factors[1]
+    scale = scale_ref[0]
+    offset = offset_ref[0]
     done = [pltpu.make_async_copy(acc.at[k], grads[k], out_sem.at[0]) for k in range(2)]
     for k in range(2):
         pl.when(odd == 1 - k)(done[k].start)
@@ -258,7 +264,6 @@
 def local(img, txt, scale, offset):
     rows, width = img.shape
     n = lax.axis_size("dp")
-    factors = jnp.concatenate([scale, offset])
     img, txt = (pltpu.with_memory_space_constraint(x, pltpu.HBM) for x in (img, txt))
     kept = pl.pallas_call(
         functools.partial(exchange, n),
@@ -268,30 +273,31 @@
             pltpu.VMEM((2, rows, width), BF16),
             pltpu.VMEM((SIZES[-1], width), F32),
         ],
-        in_specs=[SMEM] + [HBM] * 2,
+        in_specs=[SMEM] * 2 + [HBM] * 2,
         out_specs=[VMEM] * 4,
         scratch_shapes=[
             pltpu.VMEM((8, rows, width), F32),
             pltpu.VMEM((rows, rows // HALVES), F32),
             pltpu.VMEM((2, rows, rows // HALVES), BF16),
+            pltpu.SemaphoreType.REGULAR((2,)),
             pltpu.SemaphoreType.DMA((2,)),
             pltpu.SemaphoreType.DMA((6, PIECES)),
             pltpu.SemaphoreType.DMA((6, PIECES)),
         ],
         compiler_params=pltpu.CompilerParams(collective_id=0, has_side_effects=True, vmem_limit_bytes=40 * 2**20),
-    )(factors, img, txt)
+    )(scale, offset, img, txt)
     kept = [pltpu.with_memory_space_constraint(x, pltpu.VMEM) for x in kept]
     return pl.pallas_call(
         finish,
         out_shape=[jax.ShapeDtypeStruct((rows, width), F32)] * 2,
-        in_specs=[SMEM] + [VMEM] * 4,
+        in_specs=[SMEM] * 2 + [VMEM] * 4,
         out_specs=[HBM] * 2,
         scratch_shapes=[
             pltpu.VMEM((rows, width), F32),
             pltpu.SemaphoreType.DMA((5,)),
         ],
         compiler_params=pltpu.CompilerParams(vmem_limit_bytes=16 * 2**20),
-    )(factors, *kept)
+    )(scale, offset, *kept)
 
 
 def solution(mesh):

time: 94.7 us -> 91.6 us (0.967); the launches traced: 93.3 us -> 91.5 us
  Pallas kernels: 91.2 us -> 89.6 us
    pallas_call x1, Pallas kernels: 87.8 us -> 86.6 us  [local(): pl.pallas_call(functools.partial(exchange, n), out_shape=[pltpu.VMEM((2,...]
where the time goes in v2:
time: 91.6 us; the launch traced here: 91.5 us
  Pallas kernels  89.6 us (98%)
  between operations  1.93 us (2%)
    pallas_call x1, Pallas kernels, local(): pl.pallas_call(functools.partial(exchange, n), out_shape=[pltpu.VMEM((2,...  86.6 us
    pallas_call x1, Pallas kernels, local(): pl.pallas_call(finish, out_shape=[jax.ShapeDtypeStruct((rows, width), F32...  2.93 us

profile of v2, /device:TPU:0, one launch (start us, length us, event | category | flops | bytes accessed | tf_op | source)
XLA Modules:
  0.0 91.5 jit_solution(16865014064636002237)
XLA Ops:
  1.9 86.6 %shard_map.59 = (f32[2,512,1152]{2,1,0:T(8,128)S(1)}, bf16[2,512,1152]{2,1,0:T(8,128)(2,1)S(1)}, bf16[2,512,1152]{2,1,0:T(8,128)(2,1)S(1)}, f32[64,1152]{1,0:T(8,128)S(1)}) custom-call(f32[1]{0:T(128)S(6)} %copy.6.scale_ref, f32[1]{0:T(128)S(6)} %copy.7.offset_ref, f32[512,1152]{1,0:T(8,128)} %img.1, f32[512,1152]{1,0:T(8,128)} %txt.1), custom_call_target="tpu_custom_call" | custom-call | tf_op jit(solution)/shard_map/pallas_call | solution.py:268
  88.6 2.9 %shard_map.60 = (f32[512,1152]{1,0:T(8,128)}, f32[512,1152]{1,0:T(8,128)}) custom-call(f32[1]{0:T(128)S(6)} %copy.6.scale_ref, f32[1]{0:T(128)S(6)} %copy.7.offset_ref, f32[2,512,1152]{2,1,0:T(8,128)S(1)} %get-tuple-element.6.acc, bf16[2,512,1152]{2,1,0:T(8,128)(2,1)S(1)} %get-tuple-element.7.high, bf16[2,512,1152]{2,1,0:T(8,128)(2,1)S(1)} %get-tuple-element.8.low, ...), custom_call_target="tpu_custom_call" | custom-call | tf_op jit(solution)/shard_map/pallas_call | solution.py:290

commit v3 on v2

--- a/solution.py
+++ b/solution.py
@@ -16,10 +16,13 @@
 
 V, U, NEAR, A2, B2, PFB, PFA, Q3 = range(8)
 HALVES = 2
-SIZES = (64,) * 8
+LINE = 8
+LINES = 4
+SIZES = (64, 64, 64, 64, 64, 64, 80, 48)
+PART = SIZES[-1] // 2
 STARTS = tuple(sum(SIZES[:i]) for i in range(len(SIZES)))
 PIECES = len(SIZES)
-TAIL = ((0, 256, (0, 1, 2, 3)), (256, 128, (4, 5)), (384, 64, (6,)))
+TAIL = ((0, 256, (0, 1, 2, 3)), (256, 128, (4, 5)), (384, 80, (6,)))
 
 
 def split(x):
@@ -52,7 +55,7 @@
     return dot_nn(jnp.concatenate([ph, ph, pl_], axis=1), jnp.concatenate([both, xh], axis=0))
 
 
-def exchange(n, scale_ref, offset_ref, img, txt, acc, high, low, tail, buf, dots, slopes, entered, load_sem, send_sem, recv_sem):
+def exchange(n, scale_ref, offset_ref, img, txt, acc, high, low, tail, buf, dots, slopes, parked, entered, load_sem, send_sem, recv_sem, aside_send, parked_sem, passed_send, passed_recv, onward_send, onward_recv):
     rows = img.shape[0]
     half = rows // HALVES
     me = lax.axis_index("dp")
@@ -107,29 +110,142 @@
     def q3(c):
         return copy(5, c, buf.at[A2], Q3, e)
 
+    def aside():
+        return pltpu.make_async_remote_copy(
+            src_ref=txt.at[pl.ds(STARTS[-1], SIZES[-1])],
+            dst_ref=parked,
+            send_sem=aside_send,
+            recv_sem=parked_sem,
+            device_id=device(-(LINES - 1) * 2 * LINE),
+            device_id_type=MESH,
+        )
+
+    def passed():
+        return pltpu.make_async_remote_copy(
+            src_ref=parked.at[pl.ds(PART, PART)],
+            dst_ref=parked.at[pl.ds(PART, PART)],
+            send_sem=passed_send,
+            recv_sem=passed_recv,
+            device_id=device(2 * LINE),
+            device_id_type=MESH,
+        )
+
+    def onward(k):
+        return pltpu.make_async_remote_copy(
+            src_ref=parked.at[pl.ds(k * PART, PART)],
+            dst_ref=buf.at[B2, pl.ds(STARTS[-1] + k * PART, PART)],
+            send_sem=onward_send.at[k],
+            recv_sem=onward_recv.at[k],
+            device_id=device(2 + (LINES - 1 - k) * 2 * LINE),
+            device_id_type=MESH,
+        )
+
     def load(u, v):
         pltpu.make_async_copy(v, buf.at[V], load_sem.at[0]).start()
         pltpu.make_async_copy(u, buf.at[U], load_sem.at[1]).start()
 
+    z = lax.rem(me // 2, LINE)
+    first, last = z == 0, z == LINE - 1
+    above_early, below_early = z >= LINE - 2, (z >= 1) & (z <= LINE - 2)
+    one = lambda condition: condition.astype(jnp.int32)
+    is_odd, is_even = odd == 1, odd == 0
+    y = lax.rem(me // (2 * LINE), LINES)
+    detoured = is_even & last & (y == LINES - 1)
+    helper = is_even & last & (y == 0)
+    second_helper = is_even & last & (y == 1)
+    relieved = is_even & first & (y == 0)
+
+    def tell(semaphore, distance):
+        pl.semaphore_signal(semaphore, inc=1, device_id=device(distance), device_id_type=MESH)
+
+    def when(condition, do):
+        pl.when(condition)(do)
+
     barrier = pltpu.get_barrier_semaphore()
-    for distance in (-2, -1):
-        pl.semaphore_signal(barrier, inc=1, device_id=device(distance), device_id_type=MESH)
+
+    @pl.when(first | last)
+    def _():
+        tell(barrier, -2)
+        when(is_even, lambda: tell(barrier, -1))
+
+    @pl.when(z < LINE - 2)
+    def _():
+        tell(barrier, 2)
+        when(is_odd, lambda: tell(barrier, 1))
+
+    when(is_odd & (z != LINE - 1), lambda: tell(barrier, -1))
+
+    @pl.when(relieved)
+    def _():
+        for k in range(2):
+            tell(barrier, -2 - (LINES - 1 - k) * 2 * LINE)
+
+    when(helper, lambda: tell(barrier, (LINES - 1) * 2 * LINE))
+    from_below, from_above, from_core = one(below_early), one(above_early), one(z != LINE - 1)
+    signals = (1 - odd) * (from_core + 2 * from_below + from_above) + odd * (from_below + 2 * from_above)
+    signals += one(helper | second_helper | detoured)
+    when(signals > 0, lambda: pl.semaphore_wait(barrier, signals))
+
+    def send(u, v, upper):
+        for c in range(PIECES - 1):
+            (a2(c, v) if upper else b2(c, u)).start()
+        if upper:
+            a2(PIECES - 1, v).start()
+        else:
+            pl.when(jnp.logical_not(detoured))(b2(PIECES - 1, u).start)
+
+    def send_up():
+        pl.when(is_odd)(lambda: send(img, txt, True))
+        pl.when(is_even)(lambda: send(txt, img, False))
+
+    def send_down():
+        pl.when(is_odd)(lambda: send(img, txt, False))
+        pl.when(is_even)(lambda: send(txt, img, True))
+
+    @pl.when(above_early)
+    def _():
+        tell(entered.at[1], 2)
+        when(is_odd, lambda: tell(entered.at[1], 1))
+        pl.when(detoured)(aside().start)
+        send_up()
+
+    @pl.when(below_early)
+    def _():
+        tell(entered.at[0], -2)
+        when(is_even, lambda: tell(entered.at[0], -1))
+        send_down()
+
+    when(is_even & (z != LINE - 1), lambda: tell(entered.at[2], 1))
     by_core(load)
-    pl.semaphore_wait(barrier, 2)
-    for i in range(2):
-        pl.semaphore_signal(entered.at[i], inc=1, device_id=device(i + 1), device_id_type=MESH)
-
-    def send(u, v, upper):
-        for c in range(PIECES):
-            (a2(c, v) if upper else b2(c, u)).start()
-
-    pl.when(odd == 1)(lambda: send(img, txt, True))
-    pl.when(odd == 0)(lambda: send(txt, img, False))
-    for i in range(2):
-        pl.semaphore_wait(entered.at[i], 1)
-    pl.when(odd == 1)(lambda: send(img, txt, False))
-    pl.when(odd == 0)(lambda: send(txt, img, True))
+    when(helper, lambda: tell(entered.at[3], 2 + (LINES - 1) * 2 * LINE))
+    when(second_helper, lambda: tell(entered.at[3], 2 + (LINES - 2) * 2 * LINE))
+    @pl.when(z < LINE - 2)
+    def _():
+        pl.semaphore_wait(entered.at[0], 1 + odd)
+        send_up()
+
+    @pl.when(last)
+    def _():
+        pl.semaphore_wait(entered.at[1], 2 - odd)
+        send_down()
+
+    when(is_odd | last, lambda: pl.semaphore_wait(entered.at[2], 1))
     by_core(lambda u, v: near(u).start())
+
+    @pl.when(first)
+    def _():
+        pl.semaphore_wait(entered.at[1], 2 - odd)
+        send_down()
+
+        @pl.when(is_even)
+        def _():
+            tell(entered.at[2], -1)
+            tell(entered.at[2], -2)
+
+        @pl.when(relieved)
+        def _():
+            pl.semaphore_wait(entered.at[3], 2)
+            tell(entered.at[3], -2 - (LINES - 1) * 2 * LINE)
 
     acc[...] = jnp.zeros_like(acc)
     scale = scale_ref[0]
@@ -202,15 +318,40 @@
 
             @pl.when(t == 4 * h)
             def _():
+                if h == 0:
+
+                    @pl.when(helper)
+                    def _():
+                        aside().wait_recv()
+                        onward(0).start()
+                        pl.semaphore_wait(entered.at[3], 1)
+                        passed().start()
+
                 for c in pieces:
                     a2(c, txt).wait_recv()
                     q3(c).start()
                     pfa(c).start()
-                    b2(c, img).wait_recv()
+                    if c < PIECES - 1:
+                        b2(c, img).wait_recv()
+                    else:
+                        pl.when(jnp.logical_not(relieved))(b2(c, img).wait_recv)
+
+                        @pl.when(relieved)
+                        def _():
+                            for k in range(2):
+                                onward(k).wait_recv()
+
                     pfb(c).start()
 
             @pl.when(t == 4 * h + 2)
             def _():
+                if h == 0:
+
+                    @pl.when(second_helper)
+                    def _():
+                        passed().wait_recv()
+                        onward(1).start()
+
                 for c in pieces:
                     pfb(c).wait_recv()
 
@@ -231,10 +372,20 @@
     near(img).wait_send()
     for c in range(PIECES):
         a2(c, img).wait_send()
-        b2(c, img).wait_send()
+        if c < PIECES - 1:
+            b2(c, img).wait_send()
         pfb(c).wait_send()
         pfa(c).wait_send()
         q3(c).wait_send()
+    pl.when(jnp.logical_not(detoured))(b2(PIECES - 1, img).wait_send)
+    pl.when(detoured)(aside().wait_send)
+
+    @pl.when(helper)
+    def _():
+        onward(0).wait_send()
+        passed().wait_send()
+
+    pl.when(second_helper)(onward(1).wait_send)
     q3(PIECES - 1).wait_recv()
 
 
@@ -279,10 +430,17 @@
             pltpu.VMEM((8, rows, width), F32),
             pltpu.VMEM((rows, rows // HALVES), F32),
             pltpu.VMEM((2, rows, rows // HALVES), BF16),
-            pltpu.SemaphoreType.REGULAR((2,)),
+            pltpu.VMEM((SIZES[-1], width), F32),
+            pltpu.SemaphoreType.REGULAR((4,)),
             pltpu.SemaphoreType.DMA((2,)),
             pltpu.SemaphoreType.DMA((6, PIECES)),
             pltpu.SemaphoreType.DMA((6, PIECES)),
+            pltpu.SemaphoreType.DMA,
+            pltpu.SemaphoreType.DMA,
+            pltpu.SemaphoreType.DMA,
+            pltpu.SemaphoreType.DMA,
+            pltpu.SemaphoreType.DMA((2,)),
+            pltpu.SemaphoreType.DMA((2,)),
         ],
         compiler_params=pltpu.CompilerParams(collective_id=0, has_side_effects=True, vmem_limit_bytes=40 * 2**20),
     )(scale, offset, img, txt)

time: 91.6 us -> 90.9 us (level)
  no operation moved by 1% of the time
where the time goes in v3:
time: 90.9 us; the launch traced here: 90.8 us
  Pallas kernels  88.9 us (98%)
  between operations  1.93 us (2%)
    pallas_call x1, Pallas kernels, local(): pl.pallas_call(functools.partial(exchange, n), out_shape=[pltpu.VMEM((2,...  86 us
    pallas_call x1, Pallas kernels, local(): pl.pallas_call(finish, out_shape=[jax.ShapeDtypeStruct((rows, width), F32...  2.92 us

profile of v3, /device:TPU:0, one launch (start us, length us, event | category | flops | bytes accessed | tf_op | source)
XLA Modules:
  0.0 90.8 jit_solution(9908229138080481123)
XLA Ops:
  1.9 86.0 %shard_map.59 = (f32[2,512,1152]{2,1,0:T(8,128)S(1)}, bf16[2,512,1152]{2,1,0:T(8,128)(2,1)S(1)}, bf16[2,512,1152]{2,1,0:T(8,128)(2,1)S(1)}, f32[48,1152]{1,0:T(8,128)S(1)}) custom-call(f32[1]{0:T(128)S(6)} %copy.6.scale_ref, f32[1]{0:T(128)S(6)} %copy.7.offset_ref, f32[512,1152]{1,0:T(8,128)} %img.1, f32[512,1152]{1,0:T(8,128)} %txt.1), custom_call_target="tpu_custom_call" | custom-call | tf_op jit(solution)/shard_map/pallas_call | solution.py:419
  87.9 2.9 %shard_map.60 = (f32[512,1152]{1,0:T(8,128)}, f32[512,1152]{1,0:T(8,128)}) custom-call(f32[1]{0:T(128)S(6)} %copy.6.scale_ref, f32[1]{0:T(128)S(6)} %copy.7.offset_ref, f32[2,512,1152]{2,1,0:T(8,128)S(1)} %get-tuple-element.6.acc, bf16[2,512,1152]{2,1,0:T(8,128)(2,1)S(1)} %get-tuple-element.7.high, bf16[2,512,1152]{2,1,0:T(8,128)(2,1)S(1)} %get-tuple-element.8.low, ...), custom_call_target="tpu_custom_call" | custom-call | tf_op jit(solution)/shard_map/pallas_call | solution.py:448

commit v4 on v3

--- a/solution.py
+++ b/solution.py
@@ -110,13 +110,13 @@
     def q3(c):
         return copy(5, c, buf.at[A2], Q3, e)
 
-    def aside():
+    def aside(u):
         return pltpu.make_async_remote_copy(
-            src_ref=txt.at[pl.ds(STARTS[-1], SIZES[-1])],
+            src_ref=u.at[pl.ds(STARTS[-1], SIZES[-1])],
             dst_ref=parked,
             send_sem=aside_send,
             recv_sem=parked_sem,
-            device_id=device(-(LINES - 1) * 2 * LINE),
+            device_id=device(-sign * (LINES - 1) * 2 * LINE),
             device_id_type=MESH,
         )
 
@@ -126,7 +126,7 @@
             dst_ref=parked.at[pl.ds(PART, PART)],
             send_sem=passed_send,
             recv_sem=passed_recv,
-            device_id=device(2 * LINE),
+            device_id=device(sign * 2 * LINE),
             device_id_type=MESH,
         )
 
@@ -136,7 +136,7 @@
             dst_ref=buf.at[B2, pl.ds(STARTS[-1] + k * PART, PART)],
             send_sem=onward_send.at[k],
             recv_sem=onward_recv.at[k],
-            device_id=device(2 + (LINES - 1 - k) * 2 * LINE),
+            device_id=device(sign * (2 + (LINES - 1 - k) * 2 * LINE)),
             device_id_type=MESH,
         )
 
@@ -150,10 +150,12 @@
     one = lambda condition: condition.astype(jnp.int32)
     is_odd, is_even = odd == 1, odd == 0
     y = lax.rem(me // (2 * LINE), LINES)
-    detoured = is_even & last & (y == LINES - 1)
-    helper = is_even & last & (y == 0)
-    second_helper = is_even & last & (y == 1)
-    relieved = is_even & first & (y == 0)
+    sign = 1 - 2 * odd
+
+    def at(end_of_even, y_of_even):
+        return (is_even & end_of_even & (y == y_of_even)) | (is_odd & (last if end_of_even is first else first) & (y == LINES - 1 - y_of_even))
+
+    detoured, helper, second_helper, relieved = at(last, LINES - 1), at(last, 0), at(last, 1), at(first, 0)
 
     def tell(semaphore, distance):
         pl.semaphore_signal(semaphore, inc=1, device_id=device(distance), device_id_type=MESH)
@@ -175,15 +177,17 @@
 
     when(is_odd & (z != LINE - 1), lambda: tell(barrier, -1))
 
-    @pl.when(relieved)
+    @pl.when(relieved & is_even)
     def _():
         for k in range(2):
             tell(barrier, -2 - (LINES - 1 - k) * 2 * LINE)
 
-    when(helper, lambda: tell(barrier, (LINES - 1) * 2 * LINE))
+    for k, role in enumerate((helper, second_helper)):
+        when(role & is_odd, lambda: tell(barrier, -2 - (LINES - 1 - k) * 2 * LINE))
+    when(helper, lambda: tell(barrier, sign * (LINES - 1) * 2 * LINE))
     from_below, from_above, from_core = one(below_early), one(above_early), one(z != LINE - 1)
     signals = (1 - odd) * (from_core + 2 * from_below + from_above) + odd * (from_below + 2 * from_above)
-    signals += one(helper | second_helper | detoured)
+    signals += one(detoured) + (1 - odd) * one(helper | second_helper) + 2 * odd * one(relieved)
     when(signals > 0, lambda: pl.semaphore_wait(barrier, signals))
 
     def send(u, v, upper):
@@ -206,7 +210,7 @@
     def _():
         tell(entered.at[1], 2)
         when(is_odd, lambda: tell(entered.at[1], 1))
-        pl.when(detoured)(aside().start)
+        pl.when(detoured & is_even)(aside(txt).start)
         send_up()
 
     @pl.when(below_early)
@@ -217,8 +221,10 @@
 
     when(is_even & (z != LINE - 1), lambda: tell(entered.at[2], 1))
     by_core(load)
-    when(helper, lambda: tell(entered.at[3], 2 + (LINES - 1) * 2 * LINE))
-    when(second_helper, lambda: tell(entered.at[3], 2 + (LINES - 2) * 2 * LINE))
+    pl.when(detoured & is_odd)(aside(img).start)
+    for k, role in enumerate((helper, second_helper)):
+        when(role & is_even, lambda: tell(entered.at[3], 2 + (LINES - 1 - k) * 2 * LINE))
+        when(relieved & is_odd, lambda: tell(entered.at[3], 2 + (LINES - 1 - k) * 2 * LINE))
     @pl.when(z < LINE - 2)
     def _():
         pl.semaphore_wait(entered.at[0], 1 + odd)
@@ -322,9 +328,9 @@
 
                     @pl.when(helper)
                     def _():
-                        aside().wait_recv()
+                        aside(img).wait_recv()
+                        pl.semaphore_wait(entered.at[3], 1)
                         onward(0).start()
-                        pl.semaphore_wait(entered.at[3], 1)
                         passed().start()
 
                 for c in pieces:
@@ -350,6 +356,7 @@
                     @pl.when(second_helper)
                     def _():
                         passed().wait_recv()
+                        when(is_odd, lambda: pl.semaphore_wait(entered.at[3], 1))
                         onward(1).start()
 
                 for c in pieces:
@@ -378,7 +385,7 @@
         pfa(c).wait_send()
         q3(c).wait_send()
     pl.when(jnp.logical_not(detoured))(b2(PIECES - 1, img).wait_send)
-    pl.when(detoured)(aside().wait_send)
+    pl.when(detoured)(aside(img).wait_send)
 
     @pl.when(helper)
     def _():

time: 90.9 us -> 89.9 us (0.989)
  Pallas kernels: 88.9 us -> 87.3 us
    pallas_call x1, Pallas kernels: 86 us -> 84.4 us  [local(): pl.pallas_call(functools.partial(exchange, n), out_shape=[pltpu.VMEM((2,...]
where the time goes in v4:
time: 89.9 us; the launch traced here: 89.2 us
  Pallas kernels  87.3 us (97%)
  between operations  1.93 us (2%)
    pallas_call x1, Pallas kernels, local(): pl.pallas_call(functools.partial(exchange, n), out_shape=[pltpu.VMEM((2,...  84.4 us
    pallas_call x1, Pallas kernels, local(): pl.pallas_call(finish, out_shape=[jax.ShapeDtypeStruct((rows, width), F32...  2.93 us

profile of v4, /device:TPU:0, one launch (start us, length us, event | category | flops | bytes accessed | tf_op | source)
XLA Modules:
  0.0 89.2 jit_solution(17823815006519334844)
XLA Ops:
  1.9 84.4 %shard_map.59 = (f32[2,512,1152]{2,1,0:T(8,128)S(1)}, bf16[2,512,1152]{2,1,0:T(8,128)(2,1)S(1)}, bf16[2,512,1152]{2,1,0:T(8,128)(2,1)S(1)}, f32[48,1152]{1,0:T(8,128)S(1)}) custom-call(f32[1]{0:T(128)S(6)} %copy.6.scale_ref, f32[1]{0:T(128)S(6)} %copy.7.offset_ref, f32[512,1152]{1,0:T(8,128)} %img.1, f32[512,1152]{1,0:T(8,128)} %txt.1), custom_call_target="tpu_custom_call" | custom-call | tf_op jit(solution)/shard_map/pallas_call | solution.py:426
  86.3 2.9 %shard_map.60 = (f32[512,1152]{1,0:T(8,128)}, f32[512,1152]{1,0:T(8,128)}) custom-call(f32[1]{0:T(128)S(6)} %copy.6.scale_ref, f32[1]{0:T(128)S(6)} %copy.7.offset_ref, f32[2,512,1152]{2,1,0:T(8,128)S(1)} %get-tuple-element.6.acc, bf16[2,512,1152]{2,1,0:T(8,128)(2,1)S(1)} %get-tuple-element.7.high, bf16[2,512,1152]{2,1,0:T(8,128)(2,1)S(1)} %get-tuple-element.8.low, ...), custom_call_target="tpu_custom_call" | custom-call | tf_op jit(solution)/shard_map/pallas_call | solution.py:455

commit v5 on v4

--- a/solution.py
+++ b/solution.py
@@ -372,10 +372,6 @@
 
     lax.fori_loop(0, 4 * HALVES, second, 0)
 
-    for start, size, pieces in TAIL:
-        for c in pieces:
-            q3(c).wait_recv()
-        (score if size > 128 else score_small)(Q3, start, size, 1, *((False,) if size > 128 else ()))
     near(img).wait_send()
     for c in range(PIECES):
         a2(c, img).wait_send()
@@ -383,7 +379,6 @@
             b2(c, img).wait_send()
         pfb(c).wait_send()
         pfa(c).wait_send()
-        q3(c).wait_send()
     pl.when(jnp.logical_not(detoured))(b2(PIECES - 1, img).wait_send)
     pl.when(detoured)(aside(img).wait_send)
 
@@ -393,6 +388,12 @@
         passed().wait_send()
 
     pl.when(second_helper)(onward(1).wait_send)
+    for start, size, pieces in TAIL:
+        for c in pieces:
+            q3(c).wait_recv()
+        (score if size > 128 else score_small)(Q3, start, size, 1, *((False,) if size > 128 else ()))
+    for c in range(PIECES):
+        q3(c).wait_send()
     q3(PIECES - 1).wait_recv()
 
 
@@ -406,17 +407,17 @@
     for k in range(2):
         pl.when(odd == 1 - k)(done[k].start)
     xh, xl = split(tail[...])
-    step = 256
-    for m in range(0, rows, step):
+    tiles = ((0, 384), (384, 128))
+    for i, (m, step) in enumerate(tiles):
         at = pl.ds(m, step)
         result[at, :] = acc[odd, at, :] + weigh_small(scale, offset, high[odd, at, :], low[odd, at, :], xh, xl)
         for k in range(2):
-            part = pltpu.make_async_copy(result.at[at], grads[k].at[at], out_sem.at[1 + m // step])
+            part = pltpu.make_async_copy(result.at[at], grads[k].at[at], out_sem.at[1 + i])
             pl.when(odd == k)(part.start)
     done[0].wait()
-    for m in range(0, rows, step):
+    for i, (m, step) in enumerate(tiles):
         at = pl.ds(m, step)
-        pltpu.make_async_copy(result.at[at], img_grad.at[at], out_sem.at[1 + m // step]).wait()
+        pltpu.make_async_copy(result.at[at], img_grad.at[at], out_sem.at[1 + i]).wait()
 
 
 def local(img, txt, scale, offset):

time: 89.9 us -> 89.7 us (level)
  no operation moved by 1% of the time
where the time goes in v5:
time: 89.7 us; the launch traced here: 89.1 us
  Pallas kernels  87.2 us (97%)
  between operations  1.93 us (2%)
    pallas_call x1, Pallas kernels, local(): pl.pallas_call(functools.partial(exchange, n), out_shape=[pltpu.VMEM((2,...  84.4 us
    pallas_call x1, Pallas kernels, local(): pl.pallas_call(finish, out_shape=[jax.ShapeDtypeStruct((rows, width), F32...  2.78 us

profile of v5, /device:TPU:0, one launch (start us, length us, event | category | flops | bytes accessed | tf_op | source)
XLA Modules:
  0.0 89.1 jit_solution(16078472992069375754)
XLA Ops:
  1.9 84.4 %shard_map.59 = (f32[2,512,1152]{2,1,0:T(8,128)S(1)}, bf16[2,512,1152]{2,1,0:T(8,128)(2,1)S(1)}, bf16[2,512,1152]{2,1,0:T(8,128)(2,1)S(1)}, f32[48,1152]{1,0:T(8,128)S(1)}) custom-call(f32[1]{0:T(128)S(6)} %copy.6.scale_ref, f32[1]{0:T(128)S(6)} %copy.7.offset_ref, f32[512,1152]{1,0:T(8,128)} %img.1, f32[512,1152]{1,0:T(8,128)} %txt.1), custom_call_target="tpu_custom_call" | custom-call | tf_op jit(solution)/shard_map/pallas_call | solution.py:427
  86.3 2.8 %shard_map.60 = (f32[512,1152]{1,0:T(8,128)}, f32[512,1152]{1,0:T(8,128)}) custom-call(f32[1]{0:T(128)S(6)} %copy.6.scale_ref, f32[1]{0:T(128)S(6)} %copy.7.offset_ref, f32[2,512,1152]{2,1,0:T(8,128)S(1)} %get-tuple-element.6.acc, bf16[2,512,1152]{2,1,0:T(8,128)(2,1)S(1)} %get-tuple-element.7.high, bf16[2,512,1152]{2,1,0:T(8,128)(2,1)S(1)} %get-tuple-element.8.low, ...), custom_call_target="tpu_custom_call" | custom-call | tf_op jit(solution)/shard_map/pallas_call | solution.py:456
